TPU v7x, 512 devices: a whole 4x4x16 slice. The times are simulated.
512 devices in a mesh: ctx: 32 (over z, core), tp: 4 (over x), dp: 4 (over y).
Axes of the slice: x: 4, y: 4, z: 16, core: 2. Of those that a mesh axis runs over, the one named last changes fastest.
Arguments:
- attention_out: bfloat16 [8192, 4096], P('ctx', ('tp', 'dp')), may hold values from -6 to 6
- output_weight: bfloat16 [4096, 2048], P(('tp', 'dp')), may hold values from -0.09375 to 0.09375
- residual: bfloat16 [8192, 2048], P(('ctx', 'tp')), may hold values from -6 to 6
- norm_gain: float32 [2048], replicated, may hold values from 0.25 to 1.75
- routed_experts: int32 [8192, 8], P(('ctx', 'tp')), may hold values from 0 to 127, as said below
- route_weights: float32 [8192, 8], P(('ctx', 'tp')), may hold values from 0.05 to 1
- gate_weight: bfloat16 [128, 1024, 2048], P(('ctx', 'tp'), 'dp'), may hold values from -0.125 to 0.125
- up_weight: bfloat16 [128, 1024, 2048], P(('ctx', 'tp'), 'dp'), may hold values from -0.125 to 0.125
- down_weight: bfloat16 [128, 1024, 2048], P(('ctx', 'tp'), 'dp'), may hold values from -0.75 to 0.75
Outputs:
- layer_out: bfloat16 [8192, 2048], P(('ctx', 'tp', 'dp'))
Inputs may be any that keep to these rules, and one draw needn't show every extreme that they name: `routed_experts`: each row names 8 different experts. In each aligned block of 64 rows no expert is named by more than 8 rows, and one expert, the same for all blocks, is named by exactly 8 rows in every block.
All inputs are finite; a program needn't handle non-finite values.
Results may differ from a plain program's by a relative error of at most 0.009.
Values may be sent and summed in bfloat16 or wider, within the bound.
A program may use at most 64 MiB of HBM per device.

v0:
```python
import jax
import jax.numpy as jnp
from jax import lax
from jax.sharding import PartitionSpec as P

EPSILON = 1e-06
F32 = jnp.float32
BF16 = jnp.bfloat16


def on_device(
    attention_out,
    output_weight,
    residual,
    norm_gain,
    routed_experts,
    route_weights,
    gate_weight,
    up_weight,
    down_weight,
):
    rows, width = residual.shape
    top = routed_experts.shape[1]
    replicas = lax.axis_size("dp")
    quarter = rows // replicas
    replica = lax.axis_index("dp")
    experts = lax.axis_size("ctx") * lax.axis_size("tp")
    capacity = min(rows, 2 * rows * top // experts)
    share = capacity // replicas
    down_full = lax.all_gather(down_weight[0], "dp", axis=0, tiled=True)
    partial = jnp.dot(attention_out, output_weight, preferred_element_type=F32).astype(BF16)
    arrived = lax.all_to_all(
        partial.reshape(-1, quarter, width), ("tp", "dp"), split_axis=0, concat_axis=0, tiled=True
    )
    summed = jnp.sum(arrived.astype(F32), axis=0)
    own_residual = lax.dynamic_slice_in_dim(residual, replica * quarter, quarter, 0)
    own_state = own_residual.astype(F32) + summed
    square = jnp.mean(own_state * own_state, axis=-1, keepdims=True)
    own_normed = (own_state * lax.rsqrt(square + EPSILON) * norm_gain).astype(BF16)
    normed = lax.all_gather(own_normed, "dp", axis=0, tiled=True)
    flat_ids = routed_experts.reshape(-1)
    copies = flat_ids.shape[0]
    after = lax.broadcasted_iota(jnp.int32, (copies, copies), 0) > lax.broadcasted_iota(
        jnp.int32, (copies, copies), 1
    )
    before = jnp.sum(((flat_ids[:, None] == flat_ids[None, :]) & after).astype(jnp.int32), axis=1)
    local = before - replica * share
    wanted = jnp.where((local >= 0) & (local < share), flat_ids * share + local, -1)
    wanted = wanted.reshape(rows, top)
    slots = jnp.arange(experts * share, dtype=jnp.int32)
    match = wanted[:, :, None] == slots[None, None, :]
    pick = jnp.any(match, axis=1).astype(BF16)
    outgoing = lax.dot_general(pick, normed, (((0,), (0,)), ((), ())), preferred_element_type=F32)
    outgoing = outgoing.astype(BF16).reshape(experts, share, width)
    incoming = lax.all_to_all(outgoing, ("ctx", "tp"), split_axis=0, concat_axis=0, tiled=True)
    flat_rows = lax.all_gather(incoming.reshape(-1, width), "dp", axis=0, tiled=True)
    gate_act = lax.dot_general(
        flat_rows, gate_weight[0], (((1,), (1,)), ((), ())), preferred_element_type=F32
    )
    up_act = lax.dot_general(
        flat_rows, up_weight[0], (((1,), (1,)), ((), ())), preferred_element_type=F32
    )
    hidden = (jax.nn.silu(gate_act) * up_act).astype(BF16)
    hidden = lax.all_to_all(
        hidden.reshape(replicas, experts * share, -1), "dp", split_axis=0, concat_axis=0, tiled=True
    )
    hidden = jnp.moveaxis(hidden, 0, 1).reshape(experts * share, -1)
    result = jnp.dot(hidden, down_full, preferred_element_type=F32).astype(BF16)
    returned = lax.all_to_all(
        result.reshape(experts, share, width),
        ("ctx", "tp"),
        split_axis=0,
        concat_axis=0,
        tiled=True,
    ).reshape(experts * share, width)
    probs = route_weights / jnp.sum(route_weights, axis=1, keepdims=True)
    spread = jnp.sum(jnp.where(match, probs[:, :, None], 0.0), axis=1)
    high = spread.astype(BF16)
    low = (spread - high.astype(F32)).astype(BF16)
    mixed = jnp.dot(high, returned, preferred_element_type=F32) + jnp.dot(
        low, returned, preferred_element_type=F32
    )
    pieces = mixed.astype(BF16).reshape(replicas, quarter, width)
    pieces = lax.all_to_all(pieces, "dp", 0, 0, tiled=True)
    return (own_state + jnp.sum(pieces.astype(F32), axis=0)).astype(BF16)


def solution(mesh):
    in_specs = (
        P("ctx", ("tp", "dp")),
        P(("tp", "dp"), None),
        P(("ctx", "tp"), None),
        P(),
        P(("ctx", "tp"), None),
        P(("ctx", "tp"), None),
        P(("ctx", "tp"), "dp", None),
        P(("ctx", "tp"), "dp", None),
        P(("ctx", "tp"), "dp", None),
    )
    out_specs = P(("ctx", "tp", "dp"), None)
    return jax.shard_map(
        on_device, mesh=mesh, in_specs=in_specs, out_specs=out_specs, check_vma=False
    )
```

profile of v0, /device:TPU:1, one launch (start us, length us, event | category | flops | bytes accessed | tf_op | source)
XLA Modules:
  0.0 324.0 jit_solution(239269866060184144)
XLA Ops:
  6.5 1.2 copy-done
  7.8 2.3 convolution_convert_fusion
  10.1 7.6 %all-to-all-start = ((bf16[16,16,2048]{2,1,0:T(8,128)(2,1)}), bf16[16,16,2048]{2,1,0:T(8,128)(2,1)S(1)}, u32[]{:S(2)}, u32[]{:S(2)}) async-start(bf16[16,16,2048]{2,1,0:T(8,128)(2,1)} %bitcast), calls=%async_computation | async-start | bytes 2097152 | tf_op jit(solution)/shard_map/all_to_all | solution.py:32
  18.6 13.3 %all-to-all-done = bf16[16,16,2048]{2,1,0:T(8,128)(2,1)S(1)} async-done(((bf16[16,16,2048]{2,1,0:T(8,128)(2,1)}), bf16[16,16,2048]{2,1,0:T(8,128)(2,1)S(1)}, u32[]{:S(2)}, u32[]{:S(2)}) %all-to-all-start) | async-done | bytes 1048608 | tf_op jit(solution)/shard_map/all_to_all | solution.py:32
  32.3 9.4 %all_gather.9 = bf16[64,2048]{1,0:T(8,128)(2,1)S(1)} all-gather(bf16[16,2048]{1,0:T(8,128)(2,1)S(1)} %multiply_convert_fusion), channel_id=1, replica_groups=mesh['ctx'=32,'tp'=4,'dp'=4] {'dp'}, dimensions={0}, use_global_device_ids=true | all-gather | bytes 327680 | tf_op jit(solution)/shard_map/all_gather | solution.py:40
  41.7 0.5 convolution_convert_fusion.1
  42.2 0.7 reshape.52
  42.9 78.9 %all_to_all.25 = bf16[128,2,2048]{2,1,0:T(2,128)(2,1)S(1)} all-to-all(bf16[128,2,2048]{2,1,0:T(2,128)(2,1)S(1)} %reshape.52), channel_id=1, replica_groups=mesh['ctx'=32,'tp'=4,'dp'=4] {'ctx','tp'}, dimensions={0} | all-to-all | bytes 2097152 | tf_op jit(solution)/shard_map/all_to_all | solution.py:55
  121.8 1.3 reshape.53
  123.2 0.7 all-gather.6.cloned.1.call-update
  123.9 45.6 %all-gather.4.cloned.1.call-done = bf16[1024,2048]{1,0:T(8,128)(2,1)} async-done(((bf16[256,2048]{1,0:T(8,128)(2,1)}), bf16[1024,2048]{1,0:T(8,128)(2,1)}) %all-gather.4.cloned.1.call-update) | async-done | bytes 4194320 | tf_op jit(solution)/shard_map/all_gather | solution.py:56
  169.5 3.6 %fusion.8 = f32[1024,256]{1,0:T(8,128)S(1)} fusion(bf16[1024,2048]{1,0:T(8,128)(2,1)} %all-gather.4.cloned.1.call-done, bf16[1,256,2048]{2,1,0:T(8,128)(2,1)S(1)} %copy-done.6), kind=kOutput, calls=%fused_computation.11 | convolution fusion | flops 1073741824 | bytes 6291456 | tf_op jit(solution)/shard_map/dot_general | solution.py:57
  173.1 2.5 fusion.6
  175.7 1.0 copy.21
  176.7 3.5 %all-to-all-start.2 = ((bf16[4,256,256]{1,2,0:T(8,128)(2,1)}), bf16[4,256,256]{1,2,0:T(8,128)(2,1)S(1)}, u32[]{:S(2)}, u32[]{:S(2)}) async-start(bf16[4,256,256]{1,2,0:T(8,128)(2,1)} %copy.21), calls=%async_computation.2 | async-start | bytes 1048576 | tf_op jit(solution)/shard_map/all_to_all | solution.py:64
  180.1 47.8 %all-gather.6.cloned.1.call-done = bf16[1,1024,2048]{2,1,0:T(8,128)(2,1)} async-done(((bf16[1,256,2048]{2,1,0:T(8,128)(2,1)}), bf16[1,1024,2048]{2,1,0:T(8,128)(2,1)}) %all-gather.6.cloned.1.call-update) | async-done | bytes 4194320 | tf_op jit(solution)/shard_map/all_gather | solution.py:30
  228.0 3.5 %fusion.2 = bf16[256,2048]{1,0:T(8,128)(2,1)S(1)} fusion(bf16[256,1024]{0,1:T(8,128)(2,1)S(1)} %bitcast.27, bf16[1,1024,2048]{2,1,0:T(8,128)(2,1)} %all-gather.6.cloned.1.call-done), kind=kOutput, calls=%fused_computation.2 | convolution fusion | flops 1074266112 | bytes 5767168 | tf_op jit(solution)/shard_map/dot_general | solution.py:68
  231.4 1.5 reshape.56
  233.0 16.6 %all-to-all-start.3 = ((bf16[128,2,2048]{2,1,0:T(2,128)(2,1)}), bf16[128,2,2048]{2,1,0:T(2,128)(2,1)S(1)}, u32[]{:S(2)}, u32[]{:S(2)}) async-start(bf16[128,2,2048]{2,1,0:T(2,128)(2,1)} %reshape.56), calls=%async_computation.3 | async-start | bytes 2097152 | tf_op jit(solution)/shard_map/all_to_all | solution.py:69
  249.9 54.9 %all-to-all-done.3 = bf16[128,2,2048]{2,1,0:T(2,128)(2,1)S(1)} async-done(((bf16[128,2,2048]{2,1,0:T(2,128)(2,1)}), bf16[128,2,2048]{2,1,0:T(2,128)(2,1)S(1)}, u32[]{:S(2)}, u32[]{:S(2)}) %all-to-all-start.3) | async-done | bytes 1048608 | tf_op jit(solution)/shard_map/all_to_all | solution.py:69
  304.8 0.4 reshape.57
  305.6 0.3 fusion.5
  305.9 9.8 %all_to_all.26 = bf16[4,16,2048]{2,1,0:T(8,128)(2,1)S(1)} all-to-all(bf16[4,16,2048]{2,1,0:T(8,128)(2,1)S(1)} %bitcast.26), channel_id=1, replica_groups=mesh['ctx'=32,'tp'=4,'dp'=4] {'dp'}, dimensions={0} | all-to-all | bytes 524288 | tf_op jit(solution)/shard_map/all_to_all | solution.py:84
  315.7 1.5 add_convert_fusion
  (36 shorter events, 2.1 us)
Async XLA Ops:
  6.5 1.2 copy-start
  6.5 11.2 %copy-start.2 = (s32[64,8]{0,1:T(8,128)S(1)}, s32[64,8]{0,1:T(8,128)}, u32[]{:S(2)}) copy-start(s32[64,8]{0,1:T(8,128)} %param.13) | copy-start | bytes 6148
  6.5 25.5 %copy-start.1 = (bf16[64,2048]{1,0:T(8,128)(2,1)S(1)}, bf16[64,2048]{1,0:T(8,128)(2,1)}, u32[]{:S(2)}) copy-start(bf16[64,2048]{1,0:T(8,128)(2,1)} %param.11) | copy-start | bytes 786436
  6.5 25.7 %copy-start.4 = (f32[2048]{0:T(1024)S(1)}, f32[2048]{0:T(1024)}, u32[]{:S(2)}) copy-start(f32[2048]{0:T(1024)} %param.12) | copy-start | bytes 24580
  10.1 21.8 %all-to-all-start = ((bf16[16,16,2048]{2,1,0:T(8,128)(2,1)}), bf16[16,16,2048]{2,1,0:T(8,128)(2,1)S(1)}, u32[]{:S(2)}, u32[]{:S(2)}) async-start(bf16[16,16,2048]{2,1,0:T(8,128)(2,1)} %bitcast), calls=%async_computation | async-start | bytes 2097152 | tf_op jit(solution)/shard_map/all_to_all | solution.py:32
  17.7 151.8 %all-gather.4.cloned.1.call-start = ((), (), s32[]{:S(2)}) async-start(), calls=%async_computation.5 | async-start | bytes 5242880 | tf_op jit(solution)/shard_map/all_gather | solution.py:56
  121.8 47.7 %copy-start.6 = (bf16[1,256,2048]{2,1,0:T(8,128)(2,1)S(1)}, bf16[1,256,2048]{2,1,0:T(8,128)(2,1)}, u32[]{:S(2)}) copy-start(bf16[1,256,2048]{2,1,0:T(8,128)(2,1)} %param.15) | copy-start | bytes 3145732
  123.1 104.9 %all-gather.6.cloned.1.call-start = ((), (), s32[]{:S(2)}) async-start(), calls=%async_computation.6 | async-start | bytes 5242880 | tf_op jit(solution)/shard_map/all_gather | solution.py:30
  169.5 3.6 %copy-start.5 = (bf16[1024,2048]{1,0:T(8,128)(2,1)S(1)}, bf16[1024,2048]{1,0:T(8,128)(2,1)}, u32[]{:S(2)}) copy-start(bf16[1024,2048]{1,0:T(8,128)(2,1)} %all-gather.4.cloned.1.call-done) | copy-start | bytes 12582916
  176.7 51.3 %all-to-all-start.2 = ((bf16[4,256,256]{1,2,0:T(8,128)(2,1)}), bf16[4,256,256]{1,2,0:T(8,128)(2,1)S(1)}, u32[]{:S(2)}, u32[]{:S(2)}) async-start(bf16[4,256,256]{1,2,0:T(8,128)(2,1)} %copy.21), calls=%async_computation.2 | async-start | bytes 1048576 | tf_op jit(solution)/shard_map/all_to_all | solution.py:64
  228.0 21.6 %copy-start.3 = (f32[64,8]{0,1:T(8,128)S(1)}, f32[64,8]{0,1:T(8,128)}, u32[]{:S(2)}) copy-start(f32[64,8]{0,1:T(8,128)} %param.14) | copy-start | bytes 6148
  233.0 71.9 %all-to-all-start.3 = ((bf16[128,2,2048]{2,1,0:T(2,128)(2,1)}), bf16[128,2,2048]{2,1,0:T(2,128)(2,1)S(1)}, u32[]{:S(2)}, u32[]{:S(2)}) async-start(bf16[128,2,2048]{2,1,0:T(2,128)(2,1)} %reshape.56), calls=%async_computation.3 | async-start | bytes 2097152 | tf_op jit(solution)/shard_map/all_to_all | solution.py:69
Sparse Core Ops, SparseCore 0:
  123.2 46.1 all-gather.3
  171.6 56.3 all-gather.5
where the time goes:
time: 325 us; the launch traced here: 324 us
  waiting for transfers between devices  162 us (50%)
  blocking collectives  98 us (30%)
  starting transfers between devices  27.7 us (9%)
  between operations  13.6 us (4%)
  matrix products  13 us (4%)
  local copies, waits for them, and re-layouts  6.6 us (2%)
    all_to_all x1, blocking collectives, on_device(): lax.all_to_all(outgoing, ('ctx', 'tp'), split_axis=0, concat_axis=0, tile...  78.9 us
    all_to_all x1, waiting for transfers between devices, on_device(): lax.all_to_all(result.reshape(experts, share, width), ('ctx', 'tp'), spli...  54.9 us
    all_gather x1, waiting for transfers between devices, on_device(): down_full = lax.all_gather(down_weight[0], 'dp', axis=0, tiled=True)  47.8 us
    all_gather x1, waiting for transfers between devices, on_device(): lax.all_gather(incoming.reshape(-1, width), 'dp', axis=0, tiled=True)  45.6 us
    all_to_all x1, starting transfers between devices, on_device(): lax.all_to_all(result.reshape(experts, share, width), ('ctx', 'tp'), spli...  16.6 us
    all_to_all x1, waiting for transfers between devices, on_device(): lax.all_to_all(partial.reshape(-1, quarter, width), ('tp', 'dp'), split_a...  13.3 us
    all_to_all x1, blocking collectives, on_device(): pieces = lax.all_to_all(pieces, 'dp', 0, 0, tiled=True)  9.77 us
    all_gather x1, blocking collectives, on_device(): normed = lax.all_gather(own_normed, 'dp', axis=0, tiled=True)  9.37 us
  transfers between devices with their start and end apart: 5, of which 4 were waited for; matrix products, arithmetic and copies ran while one was open for 3% of the time, Pallas kernels for 0%

commit v1 on v0

--- a/solution.py
+++ b/solution.py
@@ -6,6 +6,28 @@
 EPSILON = 1e-06
 F32 = jnp.float32
 BF16 = jnp.bfloat16
+
+
+def joined_along(parts, dim):
+    parts = jnp.moveaxis(parts, 0, dim)
+    dims = parts.shape
+    return parts.reshape(*dims[:dim], dims[dim] * dims[dim + 1], *dims[dim + 2 :])
+
+
+def ring_gather(x, axis, dim):
+    size = lax.axis_size(axis)
+    pairs = [(i, (i + 1) % size) for i in range(size)]
+    back = [(b, a) for a, b in pairs]
+    lower, upper = ([], [])
+    for hop in range(size - 1):
+        if hop % 2 == 0:
+            lower.append(lax.ppermute(lower[-1] if lower else x, axis, pairs))
+        else:
+            upper.append(lax.ppermute(upper[-1] if upper else x, axis, back))
+    blocks = jnp.stack([*lower[::-1], x, *upper])
+    shift = lax.axis_index(axis) - len(lower)
+    blocks = blocks[(jnp.arange(size) - shift) % size]
+    return joined_along(blocks, dim)
 
 
 def on_device(
@@ -53,7 +75,7 @@
     outgoing = lax.dot_general(pick, normed, (((0,), (0,)), ((), ())), preferred_element_type=F32)
     outgoing = outgoing.astype(BF16).reshape(experts, share, width)
     incoming = lax.all_to_all(outgoing, ("ctx", "tp"), split_axis=0, concat_axis=0, tiled=True)
-    flat_rows = lax.all_gather(incoming.reshape(-1, width), "dp", axis=0, tiled=True)
+    flat_rows = ring_gather(incoming.reshape(-1, width), "dp", 0)
     gate_act = lax.dot_general(
         flat_rows, gate_weight[0], (((1,), (1,)), ((), ())), preferred_element_type=F32
     )

time: 325 us -> 300 us (0.923)
  blocking collectives: 98 us -> 19 us
  starting transfers between devices: 27.7 us -> 56.8 us
  waiting for transfers between devices: 162 us -> 179 us
  local copies, waits for them, and re-layouts: 6.6 us -> 12.9 us
  other arithmetic: 2.7 us -> 6.3 us
    all_to_all x1 -> x0, blocking collectives: 78.9 us -> none  [on_device(): lax.all_to_all(outgoing, ('ctx', 'tp'), split_axis=0, concat_axis=0, tile...]
    all_to_all x0 -> x1, waiting for transfers between devices: none -> 54.5 us  [on_device(): lax.all_to_all(outgoing, ('ctx', 'tp'), split_axis=0, concat_axis=0, tile...]
    all_gather x1, waiting for transfers between devices: 47.8 us -> 0.02 us  [on_device(): down_full = lax.all_gather(down_weight[0], 'dp', axis=0, tiled=True)]
    ppermute x0 -> x3, waiting for transfers between devices: none -> 47.4 us  [the longest x2 47.4 us: ring_gather(): lower.append(lax.ppermute(lower[-1] if lower else x, axis, pairs))]
    all_gather x1 -> x0, waiting for transfers between devices: 45.6 us -> none  [on_device(): lax.all_gather(incoming.reshape(-1, width), 'dp', axis=0, tiled=True)]
    all_to_all x0 -> x1, starting transfers between devices: none -> 23.8 us  [on_device(): lax.all_to_all(outgoing, ('ctx', 'tp'), split_axis=0, concat_axis=0, tile...]
    ppermute x0 -> x3, starting transfers between devices: none -> 8.39 us  [the longest x1 4.57 us: ring_gather(): upper.append(lax.ppermute(upper[-1] if upper else x, axis, back))]
    all_to_all x1, waiting for transfers between devices: 0.01 us -> 7.88 us  [on_device(): lax.all_to_all(hidden.reshape(replicas, experts * share, -1), 'dp', split...]
  transfers between devices with their start and end apart: 5 -> 8, of which waited for: 4 -> 6; matrix products, arithmetic and copies ran while one was open for 3% -> 6% of each run, Pallas kernels for 0% -> 0%
where the time goes in v1:
time: 300 us; the launch traced here: 299 us
  waiting for transfers between devices  179 us (60%)
  starting transfers between devices  56.8 us (19%)
  blocking collectives  19 us (6%)
  between operations  13.6 us (5%)
  local copies, waits for them, and re-layouts  12.9 us (4%)
  matrix products  11.8 us (4%)
  other arithmetic  6.3 us (2%)
    all_to_all x1, waiting for transfers between devices, on_device(): lax.all_to_all(result.reshape(experts, share, width), ('ctx', 'tp'), spli...  54.9 us
    all_to_all x1, waiting for transfers between devices, on_device(): lax.all_to_all(outgoing, ('ctx', 'tp'), split_axis=0, concat_axis=0, tile...  54.5 us
    ppermute x2, waiting for transfers between devices, ring_gather(): lower.append(lax.ppermute(lower[-1] if lower else x, axis, pairs))  47.4 us
    all_to_all x1, starting transfers between devices, on_device(): lax.all_to_all(outgoing, ('ctx', 'tp'), split_axis=0, concat_axis=0, tile...  23.8 us
    all_to_all x1, starting transfers between devices, on_device(): lax.all_to_all(result.reshape(experts, share, width), ('ctx', 'tp'), spli...  13.5 us
    all_to_all x1, waiting for transfers between devices, on_device(): lax.all_to_all(partial.reshape(-1, quarter, width), ('tp', 'dp'), split_a...  13.3 us
    all_to_all x1, blocking collectives, on_device(): pieces = lax.all_to_all(pieces, 'dp', 0, 0, tiled=True)  9.58 us
    all_gather x1, blocking collectives, on_device(): normed = lax.all_gather(own_normed, 'dp', axis=0, tiled=True)  9.37 us
  transfers between devices with their start and end apart: 8, of which 6 were waited for; matrix products, arithmetic and copies ran while one was open for 6% of the time, Pallas kernels for 0%

profile of v1, /device:TPU:1, one launch (start us, length us, event | category | flops | bytes accessed | tf_op | source)
XLA Modules:
  0.0 299.1 jit_solution(2491059721722903670)
XLA Ops:
  7.8 2.3 convolution_convert_fusion
  10.1 7.6 %all-to-all-start = ((bf16[16,16,2048]{2,1,0:T(8,128)(2,1)}), bf16[16,16,2048]{2,1,0:T(8,128)(2,1)S(1)}, u32[]{:S(2)}, u32[]{:S(2)}) async-start(bf16[16,16,2048]{2,1,0:T(8,128)(2,1)} %bitcast), calls=%async_computation | async-start | bytes 2097152 | tf_op jit(solution)/shard_map/all_to_all | solution.py:54
  18.6 13.3 %all-to-all-done = bf16[16,16,2048]{2,1,0:T(8,128)(2,1)S(1)} async-done(((bf16[16,16,2048]{2,1,0:T(8,128)(2,1)}), bf16[16,16,2048]{2,1,0:T(8,128)(2,1)S(1)}, u32[]{:S(2)}, u32[]{:S(2)}) %all-to-all-start) | async-done | bytes 1048608 | tf_op jit(solution)/shard_map/all_to_all | solution.py:54
  32.3 9.4 %all_gather.6 = bf16[64,2048]{1,0:T(8,128)(2,1)S(1)} all-gather(bf16[16,2048]{1,0:T(8,128)(2,1)S(1)} %multiply_convert_fusion), channel_id=1, replica_groups=mesh['ctx'=32,'tp'=4,'dp'=4] {'dp'}, dimensions={0}, use_global_device_ids=true | all-gather | bytes 327680 | tf_op jit(solution)/shard_map/all_gather | solution.py:62
  42.2 1.5 reshape.104
  43.7 23.8 %all-to-all-start.1 = ((bf16[128,2,2048]{2,1,0:T(2,128)(2,1)}), bf16[128,2,2048]{2,1,0:T(2,128)(2,1)S(1)}, u32[]{:S(2)}, u32[]{:S(2)}) async-start(bf16[128,2,2048]{2,1,0:T(2,128)(2,1)} %reshape.104), calls=%async_computation.1 | async-start | bytes 2097152 | tf_op jit(solution)/shard_map/all_to_all | solution.py:77
  68.3 54.5 %all-to-all-done.1 = bf16[128,2,2048]{2,1,0:T(2,128)(2,1)S(1)} async-done(((bf16[128,2,2048]{2,1,0:T(2,128)(2,1)}), bf16[128,2,2048]{2,1,0:T(2,128)(2,1)S(1)}, u32[]{:S(2)}, u32[]{:S(2)}) %all-to-all-start.1) | async-done | bytes 1048608 | tf_op jit(solution)/shard_map/all_to_all | solution.py:77
  124.0 1.9 collective-permute-start
  125.9 4.6 %collective-permute-start.2 = (bf16[256,2048]{1,0:T(8,128)(2,1)}, bf16[256,2048]{1,0:T(8,128)(2,1)}, u32[]{:S(2)}, u32[]{:S(2)}) collective-permute-start(bf16[256,2048]{1,0:T(8,128)(2,1)} %reshape.105), channel_id=1, source_target_pairs={{1,0},{2,1},{3,2},{0,3},{5,4},{6,5},{7,6},{4,7},{9,8},{10,9},{11,1... | collective-permute-start | bytes 3145736 | tf_op jit(solution)/shard_map/ppermute | solution.py:26
  130.5 22.1 %collective-permute-done = bf16[256,2048]{1,0:T(8,128)(2,1)} collective-permute-done((bf16[256,2048]{1,0:T(8,128)(2,1)}, bf16[256,2048]{1,0:T(8,128)(2,1)}, u32[]{:S(2)}, u32[]{:S(2)}) %collective-permute-start) | collective-permute-done | bytes 1048608 | tf_op jit(solution)/shard_map/ppermute | solution.py:24
  152.6 1.9 collective-permute-start.1
  155.0 25.3 %collective-permute-done.1 = bf16[256,2048]{1,0:T(8,128)(2,1)} collective-permute-done((bf16[256,2048]{1,0:T(8,128)(2,1)}, bf16[256,2048]{1,0:T(8,128)(2,1)}, u32[]{:S(2)}, u32[]{:S(2)}) %collective-permute-start.1) | collective-permute-done | bytes 1048608 | tf_op jit(solution)/shard_map/ppermute | solution.py:24
  180.3 3.6 %pad_maximum_fusion = bf16[4,256,2048]{2,1,0:T(8,128)(2,1)} fusion(bf16[1,256,2048]{2,1,0:T(8,128)(2,1)} %bitcast.3, bf16[1,256,2048]{2,1,0:T(8,128)(2,1)S(1)} %stack_reshape.3, bf16[1,256,2048]{2,1,0:T(8,128)(2,1)} %bitcast.2, bf16[1,256,2048]{2,1,0:T(8,128)(2,1)} %bitcast.1), kind=kLoop, calls=%fused_computation.1 | loop fusion | flops 6291456 | bytes 8388608 | tf_op jit(solution)/shard_map/stack | solution.py:27
  183.9 5.0 %gather_fusion = bf16[4,256,2048]{2,1,0:T(8,128)(2,1)} fusion(bf16[4,256,2048]{2,1,0:T(8,128)(2,1)} %pad_maximum_fusion, s32[1024]{0:T(1024)S(1)} %pad_clamp_fusion), kind=kCustom, calls=%fused_computation | custom fusion | bytes 8388624 | tf_op jit(solution)/shard_map/gather | solution.py:29
  188.9 3.6 %fusion.8 = f32[1024,256]{1,0:T(8,128)S(1)} fusion(bf16[1024,2048]{1,0:T(8,128)(2,1)} %bitcast.32, bf16[1,256,2048]{2,1,0:T(8,128)(2,1)S(1)} %copy-done.6), kind=kOutput, calls=%fused_computation.13 | convolution fusion | flops 1073741824 | bytes 6291456 | tf_op jit(solution)/shard_map/dot_general | solution.py:79
  192.7 1.3 fusion.6
  195.0 3.5 %all-to-all-start.2 = ((bf16[4,256,256]{1,2,0:T(8,128)(2,1)}), bf16[4,256,256]{1,2,0:T(8,128)(2,1)S(1)}, u32[]{:S(2)}, u32[]{:S(2)}) async-start(bf16[4,256,256]{1,2,0:T(8,128)(2,1)} %copy.21), calls=%async_computation.2 | async-start | bytes 1048576 | tf_op jit(solution)/shard_map/all_to_all | solution.py:86
  198.5 7.9 %all-to-all-done.2 = bf16[4,256,256]{1,2,0:T(8,128)(2,1)S(1)} async-done(((bf16[4,256,256]{1,2,0:T(8,128)(2,1)}), bf16[4,256,256]{1,2,0:T(8,128)(2,1)S(1)}, u32[]{:S(2)}, u32[]{:S(2)}) %all-to-all-start.2) | async-done | bytes 524320 | tf_op jit(solution)/shard_map/all_to_all | solution.py:86
  206.4 3.5 %fusion.2 = bf16[256,2048]{1,0:T(8,128)(2,1)S(1)} fusion(bf16[256,1024]{0,1:T(8,128)(2,1)S(1)} %bitcast.35, bf16[1,1024,2048]{2,1,0:T(8,128)(2,1)} %all-gather.3.cloned.1.call-done), kind=kOutput, calls=%fused_computation.4 | convolution fusion | flops 1074266112 | bytes 5767168 | tf_op jit(solution)/shard_map/dot_general | solution.py:90
  209.9 1.5 reshape.109
  211.4 13.5 %all-to-all-start.3 = ((bf16[128,2,2048]{2,1,0:T(2,128)(2,1)}), bf16[128,2,2048]{2,1,0:T(2,128)(2,1)S(1)}, u32[]{:S(2)}, u32[]{:S(2)}) async-start(bf16[128,2,2048]{2,1,0:T(2,128)(2,1)} %reshape.109), calls=%async_computation.3 | async-start | bytes 2097152 | tf_op jit(solution)/shard_map/all_to_all | solution.py:91
  225.2 54.9 %all-to-all-done.3 = bf16[128,2,2048]{2,1,0:T(2,128)(2,1)S(1)} async-done(((bf16[128,2,2048]{2,1,0:T(2,128)(2,1)}), bf16[128,2,2048]{2,1,0:T(2,128)(2,1)S(1)}, u32[]{:S(2)}, u32[]{:S(2)}) %all-to-all-start.3) | async-done | bytes 1048608 | tf_op jit(solution)/shard_map/all_to_all | solution.py:91
  281.1 9.6 %all_to_all.25 = bf16[4,16,2048]{2,1,0:T(8,128)(2,1)S(1)} all-to-all(bf16[4,16,2048]{2,1,0:T(8,128)(2,1)S(1)} %bitcast.34), channel_id=1, replica_groups=mesh['ctx'=32,'tp'=4,'dp'=4] {'dp'}, dimensions={0} | all-to-all | bytes 524288 | tf_op jit(solution)/shard_map/all_to_all | solution.py:106
  290.8 1.5 add_convert_fusion
  (47 shorter events, 7.9 us)
Async XLA Ops:
  6.5 1.2 copy-start
  6.5 11.1 %copy-start.3 = (s32[64,8]{0,1:T(8,128)S(1)}, s32[64,8]{0,1:T(8,128)}, u32[]{:S(2)}) copy-start(s32[64,8]{0,1:T(8,128)} %param.13) | copy-start | bytes 6148
  6.5 25.5 %copy-start.2 = (bf16[64,2048]{1,0:T(8,128)(2,1)S(1)}, bf16[64,2048]{1,0:T(8,128)(2,1)}, u32[]{:S(2)}) copy-start(bf16[64,2048]{1,0:T(8,128)(2,1)} %param.11) | copy-start | bytes 786436
  6.5 25.7 %copy-start.5 = (f32[2048]{0:T(1024)S(1)}, f32[2048]{0:T(1024)}, u32[]{:S(2)}) copy-start(f32[2048]{0:T(1024)} %param.12) | copy-start | bytes 24580
  10.1 21.8 %all-to-all-start = ((bf16[16,16,2048]{2,1,0:T(8,128)(2,1)}), bf16[16,16,2048]{2,1,0:T(8,128)(2,1)S(1)}, u32[]{:S(2)}, u32[]{:S(2)}) async-start(bf16[16,16,2048]{2,1,0:T(8,128)(2,1)} %bitcast), calls=%async_computation | async-start | bytes 2097152 | tf_op jit(solution)/shard_map/all_to_all | solution.py:54
  43.7 79.1 %all-to-all-start.1 = ((bf16[128,2,2048]{2,1,0:T(2,128)(2,1)}), bf16[128,2,2048]{2,1,0:T(2,128)(2,1)S(1)}, u32[]{:S(2)}, u32[]{:S(2)}) async-start(bf16[128,2,2048]{2,1,0:T(2,128)(2,1)} %reshape.104), calls=%async_computation.1 | async-start | bytes 2097152 | tf_op jit(solution)/shard_map/all_to_all | solution.py:77
  67.5 131.0 %all-gather.3.cloned.1.call-start = ((), (), s32[]{:S(2)}) async-start(), calls=%async_computation.5 | async-start | bytes 5242880 | tf_op jit(solution)/shard_map/all_gather | solution.py:52
  124.0 28.6 %collective-permute-start = (bf16[256,2048]{1,0:T(8,128)(2,1)}, bf16[256,2048]{1,0:T(8,128)(2,1)}, u32[]{:S(2)}, u32[]{:S(2)}) collective-permute-start(bf16[256,2048]{1,0:T(8,128)(2,1)} %reshape.105), channel_id=1, source_target_pairs={{0,1},{1,2},{2,3},{3,0},{4,5},{5,6},{6,7},{7,4},{8,9},{9,10},{10,1... | collective-permute-start | bytes 3145736 | tf_op jit(solution)/shard_map/ppermute | solution.py:24
  125.9 29.0 %collective-permute-start.2 = (bf16[256,2048]{1,0:T(8,128)(2,1)}, bf16[256,2048]{1,0:T(8,128)(2,1)}, u32[]{:S(2)}, u32[]{:S(2)}) collective-permute-start(bf16[256,2048]{1,0:T(8,128)(2,1)} %reshape.105), channel_id=1, source_target_pairs={{1,0},{2,1},{3,2},{0,3},{5,4},{6,5},{7,6},{4,7},{9,8},{10,9},{11,1... | collective-permute-start | bytes 3145736 | tf_op jit(solution)/shard_map/ppermute | solution.py:26
  152.6 27.7 %collective-permute-start.1 = (bf16[256,2048]{1,0:T(8,128)(2,1)}, bf16[256,2048]{1,0:T(8,128)(2,1)}, u32[]{:S(2)}, u32[]{:S(2)}) collective-permute-start(bf16[256,2048]{1,0:T(8,128)(2,1)} %collective-permute-done), channel_id=1, source_target_pairs={{0,1},{1,2},{2,3},{3,0},{4,5},{5,6},{6,7},{7,4},{8,9},{9,10},{10,1... | collective-permute-start | bytes 3145736 | tf_op jit(solution)/shard_map/ppermute | solution.py:24
  183.9 5.1 %copy-start.6 = (bf16[1,256,2048]{2,1,0:T(8,128)(2,1)S(1)}, bf16[1,256,2048]{2,1,0:T(8,128)(2,1)}, u32[]{:S(2)}) copy-start(bf16[1,256,2048]{2,1,0:T(8,128)(2,1)} %param.15) | copy-start | bytes 3145732
  188.9 3.6 %copy-start.1 = (bf16[4,256,2048]{2,1,0:T(8,128)(2,1)S(1)}, bf16[4,256,2048]{2,1,0:T(8,128)(2,1)}, u32[]{:S(2)}) copy-start(bf16[4,256,2048]{2,1,0:T(8,128)(2,1)} %gather_fusion) | copy-start | bytes 12582916
  188.9 3.7 %copy-start.7 = (bf16[1,256,2048]{2,1,0:T(8,128)(2,1)S(1)}, bf16[1,256,2048]{2,1,0:T(8,128)(2,1)}, u32[]{:S(2)}) copy-start(bf16[1,256,2048]{2,1,0:T(8,128)(2,1)} %param.16) | copy-start | bytes 3145732
  195.0 11.4 %all-to-all-start.2 = ((bf16[4,256,256]{1,2,0:T(8,128)(2,1)}), bf16[4,256,256]{1,2,0:T(8,128)(2,1)S(1)}, u32[]{:S(2)}, u32[]{:S(2)}) async-start(bf16[4,256,256]{1,2,0:T(8,128)(2,1)} %copy.21), calls=%async_computation.2 | async-start | bytes 1048576 | tf_op jit(solution)/shard_map/all_to_all | solution.py:86
  206.4 18.5 %copy-start.4 = (f32[64,8]{0,1:T(8,128)S(1)}, f32[64,8]{0,1:T(8,128)}, u32[]{:S(2)}) copy-start(f32[64,8]{0,1:T(8,128)} %param.14) | copy-start | bytes 6148
  211.4 68.7 %all-to-all-start.3 = ((bf16[128,2,2048]{2,1,0:T(2,128)(2,1)}), bf16[128,2,2048]{2,1,0:T(2,128)(2,1)S(1)}, u32[]{:S(2)}, u32[]{:S(2)}) async-start(bf16[128,2,2048]{2,1,0:T(2,128)(2,1)} %reshape.109), calls=%async_computation.3 | async-start | bytes 2097152 | tf_op jit(solution)/shard_map/all_to_all | solution.py:91
Sparse Core Ops, SparseCore 0:
  70.5 55.2 all-gather.2
